TPU v7x, 256 devices: a whole 4x4x8 slice. The times are simulated.
256 devices in a mesh: ctx: 16 (over z, x_lo), head: 16 (over x_hi, y, core).
Axes of the slice: x: 4 (x_hi: 2, x_lo: 2; x = x_hi * 2 + x_lo), y: 4, z: 8, core: 2. Of those that a mesh axis runs over, the one named last changes fastest.
Arguments:
- queries: bfloat16 [2048, 24576], P('ctx', 'head'), may hold values from -20 to 20
- compressed: bfloat16 [2048, 576], P('ctx'), may hold values from -60 to 60
- kv_up: bfloat16 [512, 32768], P(None, 'head'), may hold values from -0.25 to 0.25
- w_out: bfloat16 [16384, 7168], P('head', 'ctx'), may hold values from -0.046875 to 0.046875
- positions: int32 [2048], P('ctx'), may hold values from 0 to 2047, as said below
- latent_gain: float32 [512], replicated, may hold values from 0.1 to 1.9
Outputs:
- layer_out: bfloat16 [2048, 7168], P('head', 'ctx')
Inputs may be any that keep to these rules, and one draw needn't show every extreme that they name: A permutation of 0 to 2047 made of runs of 64 consecutive positions, each run starting at a multiple of 64.
All inputs are finite; a program needn't handle non-finite values.
Results may differ from a plain program's by a relative error of at most 0.02.
Values may be sent and summed in bfloat16 or wider, within the bound.
A program may use at most 128 MiB of HBM per device.

v0:
```python
import math

import jax
import jax.numpy as jnp
from jax import lax
from jax.sharding import PartitionSpec as P

LAT = 512
NOPE = 128
VD = 128
QK = 192


def per_device(queries, compressed, kv_up, w_out, positions, latent_gain):
    tok_rows = queries.shape[0]
    head_count = kv_up.shape[1] // (NOPE + VD)
    query_all = queries.reshape(tok_rows, head_count, QK)
    query_nope = query_all[:, :, :NOPE]
    query_rope = query_all[:, :, NOPE:]
    latent = compressed[:, :LAT].astype(jnp.float32)
    normed = (
        latent * lax.rsqrt(jnp.mean(latent * latent, axis=-1, keepdims=True) + 1e-06) * latent_gain
    ).astype(jnp.bfloat16)
    rope_keys = compressed[:, LAT:]
    score_scale = 1.0 / math.sqrt(QK)
    packed = jnp.concatenate([normed, rope_keys], axis=1)
    pieces = (
        lax.all_gather(packed, "ctx", axis=0, tiled=True),
        lax.all_gather(positions, "ctx", axis=0, tiled=True),
    )
    key_positions = pieces[1]
    row_count = pieces[0].shape[0]
    expanded = jnp.dot(pieces[0][:, :LAT], kv_up, preferred_element_type=jnp.float32).astype(
        jnp.bfloat16
    )
    expanded = expanded.reshape(row_count, head_count, NOPE + VD)
    key_nope = expanded[:, :, :NOPE]
    values = expanded[:, :, NOPE:]
    rope_piece = pieces[0][:, LAT:]
    running = jnp.full((tok_rows, head_count), -1e30, jnp.float32)
    scores = jnp.einsum("qhd,khd->qhk", query_nope, key_nope, preferred_element_type=jnp.float32)
    scores = scores + jnp.einsum(
        "qhd,kd->qhk", query_rope, rope_piece, preferred_element_type=jnp.float32
    )
    scores = scores * score_scale
    visible = key_positions[None, None, :] <= positions[:, None, None]
    scores = jnp.where(visible, scores, jnp.float32(-1e30))
    updated = jnp.maximum(running, jnp.max(scores, axis=-1))
    weights = jnp.exp(scores - updated[:, :, None])
    totals = jnp.sum(weights, axis=-1)
    numerator = jnp.einsum(
        "qhk,khd->qhd", weights.astype(jnp.bfloat16), values, preferred_element_type=jnp.float32
    )
    final_state = (updated, totals, numerator)
    running, totals, numerator = final_state
    attended = (
        (numerator / totals[:, :, None]).astype(jnp.bfloat16).reshape(tok_rows, head_count * VD)
    )
    gathered = lax.all_gather(attended, "ctx", axis=0, tiled=True)
    return lax.psum_scatter(
        jnp.dot(gathered, w_out, preferred_element_type=jnp.float32).astype(jnp.bfloat16),
        "head",
        scatter_dimension=0,
        tiled=True,
    )


def solution(mesh):
    in_specs = (P("ctx", "head"), P("ctx", None), P(None, "head"), P("head", "ctx"), P("ctx"), P())
    out_specs = P("head", "ctx")
    return jax.shard_map(
        per_device, mesh=mesh, in_specs=in_specs, out_specs=out_specs, check_vma=False
    )
```

profile of v0, /device:TPU:6, one launch (start us, length us, event | category | flops | bytes accessed | tf_op | source)
XLA Modules:
  0.0 332.9 jit_solution(15235141149769840983)
XLA Ops:
  6.5 1.1 fusion.26
  7.7 0.7 slice.25
  8.4 1.1 fusion.28
  9.5 0.7 pad_maximum_fusion
  10.1 0.0 all-gather.4.cloned.1.call-update
  10.1 0.0 all-gather.6.cloned.1.call-start
  10.2 1.2 copy.15
  11.4 33.5 %all-gather = s32[16,1,128]{2,1,0:T(1,128)S(1)} all-gather(s32[1,1,128]{2,1,0:T(1,128)} %bitcast.34), channel_id=1, replica_groups=mesh['ctx'=16,'head'=16] {'ctx'}, dimensions={0}, use_global_device_ids=true | all-gather | bytes 8704 | tf_op jit(solution)/shard_map/all_gather | solution.py:29
  44.9 1.0 broadcast_compare_fusion
  45.9 55.3 %all-gather.4.cloned.1.call-done = bf16[2048,576]{0,1:T(8,128)(2,1)} async-done(((bf16[128,576]{0,1:T(8,128)(2,1)}), bf16[2048,576]{0,1:T(8,128)(2,1)}) %all-gather.4.cloned.1.call-update) | async-done | bytes 2359312 | tf_op jit(solution)/shard_map/all_gather | solution.py:28
  101.2 6.4 %convolution_convert_fusion = bf16[2048,2048]{0,1:T(8,128)(2,1)S(1)} fusion(bf16[512,2048]{1,0:T(8,128)(2,1)S(1)} %copy-done, bf16[2048,576]{0,1:T(8,128)(2,1)} %all-gather.4.cloned.1.call-done), kind=kOutput, calls=%fused_computation.4 | convolution fusion | flops 4299161600 | bytes 12582912 | tf_op jit(solution)/shard_map/dot_general | solution.py:33
  107.6 1.4 fusion.6
  109.1 2.7 fusion.31
  111.8 1.1 fusion.2
  112.9 0.0 copy-start.1
  112.9 2.5 fusion.21
  115.4 0.0 all-gather.6.cloned.1.call-update
  115.4 0.0 reduce-scatter.4.cloned.1.call-start
  115.5 118.4 %all-gather.6.cloned.1.call-done = bf16[2048,1024]{0,1:T(8,128)(2,1)} async-done(((bf16[128,1024]{0,1:T(8,128)(2,1)}), bf16[2048,1024]{0,1:T(8,128)(2,1)}) %all-gather.6.cloned.1.call-update) | async-done | bytes 4194320 | tf_op jit(solution)/shard_map/all_gather | solution.py:59
  233.9 5.5 %convolution_convert_fusion.1 = bf16[2048,448]{0,1:T(8,128)(2,1)} fusion(bf16[1024,448]{0,1:T(8,128)(2,1)S(1)} %copy-done.1, bf16[2048,1024]{0,1:T(8,128)(2,1)} %all-gather.6.cloned.1.call-done), kind=kOutput, calls=%fused_computation.12 | convolution fusion | flops 1879965696 | bytes 6946816 | tf_op jit(solution)/shard_map/dot_general | solution.py:61
  239.4 3.8 %copy.19 = bf16[2048,448]{1,0:T(8,128)(2,1)} copy(bf16[2048,448]{0,1:T(8,128)(2,1)} %convolution_convert_fusion.1) | data formatting | bytes 3670016
  243.2 0.0 reduce-scatter.4.cloned.1.call-update
  243.3 81.4 %reduce-scatter.4.cloned.1.call-done = bf16[128,448]{1,0:T(8,128)(2,1)} async-done(((bf16[2048,448]{1,0:T(8,128)(2,1)}), bf16[128,448]{1,0:T(8,128)(2,1)}) %reduce-scatter.4.cloned.1.call-update) | async-done | bytes 114704
  324.7 1.7 copy.20
  (6 shorter events, 0.0 us)
Async XLA Ops:
  6.5 94.7 %copy-start = (bf16[512,2048]{1,0:T(8,128)(2,1)S(1)}, bf16[512,2048]{1,0:T(8,128)(2,1)}, u32[]{:S(2)}) copy-start(bf16[512,2048]{1,0:T(8,128)(2,1)} %param.8) | copy-start | bytes 6291460
  6.5 94.7 %all-gather.4.cloned.1.call-start = ((), (), s32[]{:S(2)}) async-start(), calls=%async_computation.1 | async-start | bytes 2506752 | tf_op jit(solution)/shard_map/all_gather | solution.py:28
  10.1 223.8 %all-gather.6.cloned.1.call-start = ((), (), s32[]{:S(2)}) async-start(), calls=%async_computation.2 | async-start | bytes 4456448 | tf_op jit(solution)/shard_map/all_gather | solution.py:59
  112.9 121.0 %copy-start.1 = (bf16[1024,448]{0,1:T(8,128)(2,1)S(1)}, bf16[1024,448]{0,1:T(8,128)(2,1)}, u32[]{:S(2)}) copy-start(bf16[1024,448]{0,1:T(8,128)(2,1)} %param.9) | copy-start | bytes 2752516
  115.4 209.2 %reduce-scatter.4.cloned.1.call-start = ((), (), s32[]{:S(2)}) async-start(), calls=%async_computation.3 | async-start | bytes 2228224
Sparse Core Ops, SparseCore 0:
  10.3 90.9 all-gather.3
  115.6 118.2 all-gather.5
  243.4 81.2 reduce-scatter.3
where the time goes:
time: 334 us; the launch traced here: 333 us
  waiting for transfers between devices  255 us (76%)
  blocking collectives  33.5 us (10%)
  matrix products  18.5 us (6%)
  between operations  13.2 us (4%)
  local copies, waits for them, and re-layouts  7.43 us (2%)
  other arithmetic  4.97 us (1%)
    all_gather x1, waiting for transfers between devices, per_device(): gathered = lax.all_gather(attended, 'ctx', axis=0, tiled=True)  118 us
    unnamed x4, waiting for transfers between devices  81.4 us
    all_gather x1, waiting for transfers between devices, per_device(): lax.all_gather(packed, 'ctx', axis=0, tiled=True)  55.3 us
    all_gather x1, blocking collectives, per_device(): lax.all_gather(positions, 'ctx', axis=0, tiled=True)  33.5 us
    unnamed x7, local copies, waits for them, and re-layouts  6.72 us
  transfers between devices with their start and end apart: 3, of which 3 were waited for; matrix products, arithmetic and copies ran while one was open for 1% of the time, Pallas kernels for 0%

commit v1 on v0

v1 whole, which is shorter than its diff:
```python
import math

import jax
import jax.numpy as jnp
from jax import lax
from jax.experimental import pallas as pl
from jax.experimental.pallas import tpu as pltpu
from jax.sharding import PartitionSpec as P

LAT = 512
NOPE = 128
ROPE = 64
VD = 128
QK = 192
WIDE = 640
ROWS = 128
HEADS_DEV = 8
CHUNKS = 4
NZ = 8
COLS = 448
MESH = pl.DeviceIdType.MESH
SCALE = 1.0 / math.sqrt(QK)
NT = (((1,), (1,)), ((), ()))


def kernel(
    q_hbm, comp_ref, kv_hbm, w_hbm, pos_ref, gain_ref, out_ref,
    packed, qcat, q_in, kv_in, kv_t, keys, vals_t, bias, att, full, w_buf, part, got1, sum1, got2, sum2, result,
    p1_send, p1_recv, p1s_send, p1s_recv, pair_send, pair_recv, w_send, w_recv, load_sem,
    ring_send, ring_recv, sib_send, sib_recv, swap_send, swap_recv,
    first_send, first_recv, second_send, second_recv, last_send, last_recv,
):
    ctx, head = lax.axis_index("ctx"), lax.axis_index("head")
    z, a = ctx // 2, ctx % 2
    xh, y, b = head // 8, (head // 2) % 4, head % 2
    x = xh * 2 + a
    diagonal = a == b
    partner = (z * 2 + b, xh * 8 + y * 2 + a)
    sibling = (ctx, xh * 8 + y * 2 + (1 - b))

    def along_z(d):
        return (((z + d + NZ) % NZ) * 2 + a, head)

    def in_plane(px, py, core):
        return (z * 2 + px % 2, (px // 2) * 8 + py * 2 + core)

    def block(dz, core):
        return ((z + dz + 2 * NZ) % NZ) * 2 + core

    def rows(blk):
        return pl.ds(pl.multiple_of(blk * ROWS, ROWS), ROWS)

    def remote(src, dst, send, recv, device):
        return pltpu.make_async_remote_copy(
            src_ref=src, dst_ref=dst, send_sem=send, recv_sem=recv, device_id=device, device_id_type=MESH
        )

    kv_load = pltpu.make_async_copy(kv_hbm, kv_in, load_sem.at[0])
    q_load = pltpu.make_async_copy(q_hbm, q_in, load_sem.at[1])
    kv_load.start()
    q_load.start()

    bar = pltpu.get_barrier_semaphore()

    def greet(k, carry):
        n = (a * 16 + head + k) % 32
        pl.semaphore_signal(bar, inc=1, device_id=(z * 2 + n // 16, n % 16), device_id_type=MESH)
        return carry

    lax.fori_loop(1, 32, greet, 0)
    for d in (1, -1):
        pl.semaphore_signal(bar, inc=1, device_id=along_z(d), device_id_type=MESH)

    latent = comp_ref[:, :LAT].astype(jnp.float32)
    normed = latent * lax.rsqrt(jnp.mean(latent * latent, axis=-1, keepdims=True) + 1e-06) * gain_ref[...]
    own = rows(ctx)
    packed[own, :LAT] = normed.astype(jnp.bfloat16)
    pos = pos_ref[...]
    high = jnp.broadcast_to((pos >> 6).astype(jnp.float32), (ROWS, ROWS)).T
    low = jnp.broadcast_to((pos & 63).astype(jnp.float32), (ROWS, ROWS)).T
    lane = lax.broadcasted_iota(jnp.int32, (ROWS, ROWS), 1)
    rope = comp_ref[:, LAT:].astype(jnp.float32)
    rope = jnp.concatenate([rope, rope], axis=1)
    tail = jnp.where(lane < 64, rope, jnp.where(lane < 96, high, low))
    packed[own, LAT:] = tail.astype(jnp.bfloat16)

    pl.semaphore_wait(bar, 33)

    pair = remote(packed.at[own], packed.at[own], pair_send, pair_recv, partner)
    w_swap = remote(w_hbm, w_buf, w_send, w_recv, partner)
    w_load = pltpu.make_async_copy(w_hbm, w_buf, load_sem.at[2])

    def p1_ring(i, s):
        d = 1 if i == 0 else -1
        part_rows = rows(block(-d * (s - 1), b))
        return remote(packed.at[part_rows], packed.at[part_rows], p1_send.at[i, s - 1], p1_recv.at[i, s - 1], along_z(d))

    def p1_half(i):
        d = 1 if i == 0 else -1
        half = pl.ds(pl.multiple_of(block(-d * 3, b) * ROWS + i * 64, 64), 64)
        return remote(packed.at[half], packed.at[half], p1_send.at[i, 3], p1_recv.at[i, 3], along_z(d))

    def p1_sib(i, s):
        d = 1 if i == 0 else -1
        part_rows = rows(block(-d * s, b))
        return remote(packed.at[part_rows], packed.at[part_rows], p1s_send.at[i, s], p1s_recv.at[i, s], sibling)

    @pl.when(jnp.logical_not(diagonal))
    def _():
        pair.start()
        w_swap.start()

    @pl.when(diagonal)
    def _():
        w_load.start()
        p1_ring(0, 1).start()
        p1_ring(1, 1).start()

    kv_load.wait()
    for h in range(HEADS_DEV):
        kv_t[h] = kv_in[:, h * 256 + NOPE : (h + 1) * 256].astype(jnp.float32).T.astype(jnp.bfloat16)
    q_load.wait()
    for j in range(HEADS_DEV // 2):
        first = q_in[:, j * 384 : j * 384 + 128]
        second = q_in[:, j * 384 + 128 : j * 384 + 256].astype(jnp.float32)
        third = q_in[:, j * 384 + 256 : j * 384 + 384].astype(jnp.float32)
        second_turned = pltpu.roll(second, 64, 1)
        third_turned = pltpu.roll(third, 64, 1)
        qcat[2 * j, :, :NOPE] = first
        qcat[2 * j, :, NOPE:] = jnp.where(lane < 64, second, 0.0).astype(jnp.bfloat16)
        qcat[2 * j + 1, :, :NOPE] = jnp.where(lane < 64, second_turned, third_turned).astype(jnp.bfloat16)
        qcat[2 * j + 1, :, NOPE:] = jnp.where(lane < 64, third_turned, 0.0).astype(jnp.bfloat16)

    def expand(blk0, blk1):
        both = jnp.concatenate([packed[rows(blk0), :LAT], packed[rows(blk1), :LAT]], axis=0)

        def heads(hp, carry):
            k_cols = jnp.concatenate(
                [kv_in[:, pl.ds(pl.multiple_of(hp * 512 + i * 256, 256), NOPE)] for i in (0, 1)], axis=1
            )
            k = jnp.dot(both, k_cols, preferred_element_type=jnp.float32).astype(jnp.bfloat16)
            v_rows = jnp.concatenate([kv_t[hp * 2], kv_t[hp * 2 + 1]], axis=0)
            v = lax.dot_general(v_rows, both, NT, preferred_element_type=jnp.float32).astype(jnp.bfloat16)
            for i in (0, 1):
                for j, blk in ((0, blk0), (1, blk1)):
                    keys[hp * 2 + i, rows(blk), :] = k[j * 128 : j * 128 + 128, i * 128 : i * 128 + 128]
                    vals_t[hp * 2 + i, :, rows(blk)] = v[i * 128 : i * 128 + 128, j * 128 : j * 128 + 128]
            return carry

        lax.fori_loop(0, HEADS_DEV // 2, heads, 0)
        for blk in (blk0, blk1):
            extra = packed[rows(blk), LAT:].astype(jnp.float32)
            key_pos = extra[:, 64:65] * 64.0 + extra[:, 96:97]
            visible = key_pos <= pos.astype(jnp.float32)
            bias[rows(blk), :] = jnp.where(visible, 0.0, -1e30)

    @pl.when(jnp.logical_not(diagonal))
    def _():
        pair.wait_recv()
        p1_ring(0, 1).start()
        p1_ring(1, 1).start()
        p1_sib(0, 0).start()

    @pl.when(diagonal)
    def _():
        p1_sib(0, 0).wait_recv()

    expand(block(0, 0), block(0, 1))

    def p1_step(s, carry):
        for i in (0, 1):
            p1_ring(i, s).wait_recv()
            p1_sib(i, s).start()

            @pl.when(s < 3)
            def _():
                p1_ring(i, s + 1).start()

            @pl.when(s == 3)
            def _():
                p1_half(i).start()

        expand(block(-s, b), block(s, b))

        @pl.when(s > 1)
        def _():
            for i in (0, 1):
                p1_sib(i, s - 1).wait_recv()
            expand(block(1 - s, 1 - b), block(s - 1, 1 - b))

        return carry

    lax.fori_loop(1, 4, p1_step, 0)
    for i in (0, 1):
        p1_half(i).wait_recv()
    p1_sib(0, 4).start()
    for i in (0, 1):
        p1_sib(i, 3).wait_recv()
    expand(block(-3, 1 - b), block(3, 1 - b))
    p1_sib(0, 4).wait_recv()
    expand(block(4, 0), block(4, 1))

    def attend(h):
        k = jnp.concatenate([keys[h], packed[:, LAT:]], axis=1)
        s = lax.dot_general(k, qcat[h], NT, preferred_element_type=jnp.float32)
        s = s * SCALE + bias[...]
        e = jnp.exp(s - jnp.max(s, axis=0, keepdims=True))
        total = jnp.sum(e, axis=0, keepdims=True)
        o = jnp.dot(vals_t[h], e.astype(jnp.bfloat16), preferred_element_type=jnp.float32)
        return (o / total).T.astype(jnp.bfloat16)

    def ring(i, p, s):
        d = 1 if i == 0 else -1
        r = rows(block(-d * (s - 1), b))
        return remote(full.at[p, r], full.at[p, r], ring_send.at[i, p, s - 1], ring_recv.at[i, p, s - 1], along_z(d))

    def sib(p, n, dz):
        r = rows(block(dz, b))
        return remote(full.at[p, r], full.at[p, r], sib_send.at[p, n], sib_recv.at[p, n], sibling)

    def swap(p):
        return remote(att.at[p], full.at[p, own], swap_send.at[p], swap_recv.at[p], partner)

    def sib_of(p, i, s):
        d = 1 if i == 0 else -1
        return sib(p, i * 3 + s, -d * s)

    def pass_on(p, s):
        @pl.when(s < 4)
        def _():
            for i in (0, 1):
                ring(i, p, s).wait_recv()
                sib_of(p, i, s).start()

                @pl.when((s < 3) | ((p < 2) if i == 0 else (p >= 2)))
                def _():
                    ring(i, p, s + 1).start()

        @pl.when(s == 4)
        def _():
            for i in (0, 1):
                @pl.when((p < 2) if i == 0 else (p >= 2))
                def _():
                    ring(i, p, 4).wait_recv()
            sib(p, 7, 4).start()

    def early(t, carry):
        for i in (0, 1):
            att[t, :, i * VD : (i + 1) * VD] = attend(2 * t + i)

        @pl.when(diagonal)
        def _():
            full[t, own, :] = att[t]

        @pl.when(jnp.logical_not(diagonal))
        def _():
            swap(t).start()
            swap(t).wait_recv()

        ring(0, t, 1).start()
        ring(1, t, 1).start()
        sib(t, 0, 0).start()

        def older(p, c):
            pass_on(p, t - p)
            return c

        lax.fori_loop(0, t, older, 0)
        return carry

    lax.fori_loop(0, CHUNKS, early, 0)

    u = jnp.where(b == 0, y, x)
    v = jnp.where(b == 0, x, y)

    def first_copy(n, j):
        t = (u + j) % 4
        device = in_plane(jnp.where(b == 0, x, t), jnp.where(b == 0, t, y), b)
        src = part.at[n, pl.ds(pl.multiple_of(t * 64, 64), 64)]
        return remote(src, got1.at[n, j - 1], first_send.at[n, j - 1], first_recv.at[n, j - 1], device)

    def second_copy(n, j):
        t = (v + j) % 4
        device = in_plane(jnp.where(b == 0, t, x), jnp.where(b == 0, y, t), b)
        src = sum1.at[n, pl.ds(pl.multiple_of(t * 16, 16), 16)]
        return remote(src, got2.at[n, j - 1], second_send.at[n, j - 1], second_recv.at[n, j - 1], device)

    def far(n):
        return (z + jnp.where(n % 2 == 1, -((n + 1) // 2), n // 2) + NZ) % NZ

    def project(n, carry):
        zp = far(n)
        for i in (0, 1):
            r = rows(zp * 2 + i)
            lhs = jnp.concatenate([full[p, r, :] for p in range(CHUNKS)], axis=1)
            part[n, i * ROWS : (i + 1) * ROWS, :] = jnp.dot(
                lhs, w_buf[...], preferred_element_type=jnp.float32
            ).astype(jnp.bfloat16)
        for j in (1, 2, 3):
            first_copy(n, j).start()
        return carry

    def sum_first(n, carry):
        total = part[n, pl.ds(pl.multiple_of(u * 64, 64), 64), :].astype(jnp.float32)
        for j in (1, 2, 3):
            first_copy(n, j).wait_recv()
        for j in (1, 2, 3):
            total = total + got1[n, j - 1].astype(jnp.float32)
        sum1[n] = total.astype(jnp.bfloat16)
        for j in (1, 2, 3):
            second_copy(n, j).start()
        return carry

    slot = (u % 2) * 4 + v

    def last_copy(n):
        zp = far(n)
        device = in_plane((zp // 4) * 2 + b, zp % 4, u // 2)
        return remote(
            sum2.at[n], result.at[pl.ds(pl.multiple_of(slot * 16, 16), 16)], last_send.at[n], last_recv.at[slot], device
        )

    def stays(n):
        zp = far(n)
        return diagonal & (u // 2 == b) & (zp == xh * 4 + y)

    def sum_second(n, carry):
        total = sum1[n, pl.ds(pl.multiple_of(v * 16, 16), 16), :].astype(jnp.float32)
        for j in (1, 2, 3):
            second_copy(n, j).wait_recv()
        for j in (1, 2, 3):
            total = total + got2[n, j - 1].astype(jnp.float32)
        sum2[n] = total.astype(jnp.bfloat16)

        @pl.when(stays(n))
        def _():
            result[pl.ds(pl.multiple_of(slot * 16, 16), 16), :] = sum2[n]

        @pl.when(jnp.logical_not(stays(n)))
        def _():
            last_copy(n).start()

        return carry

    def sib_wait(i, s):
        for p in range(CHUNKS):
            sib_of(p, i, s).wait_recv()

    @pl.when(diagonal)
    def _():
        w_load.wait()

    @pl.when(jnp.logical_not(diagonal))
    def _():
        w_swap.wait_recv()

    def pass_all(t):
        def older(p, c):
            pass_on(p, t - p)
            return c

        lax.fori_loop(max(0, t - 4), CHUNKS, older, 0)

    pass_all(4)
    for p in range(CHUNKS):
        sib(p, 0, 0).wait_recv()
    project(0, 0)
    for i in (0, 1):
        sib_wait(i, 1)
    lax.fori_loop(1, 3, project, 0)
    pass_all(5)
    for i in (0, 1):
        sib_wait(i, 2)
    lax.fori_loop(3, 5, project, 0)
    lax.fori_loop(0, 3, sum_first, 0)
    pass_all(6)
    for i in (0, 1):
        sib_wait(i, 3)
    lax.fori_loop(5, 7, project, 0)
    lax.fori_loop(3, 5, sum_first, 0)
    lax.fori_loop(0, 3, sum_second, 0)
    pass_all(7)
    for p in range(CHUNKS):
        sib(p, 7, 4).wait_recv()
    project(7, 0)
    lax.fori_loop(5, 7, sum_first, 0)
    lax.fori_loop(3, 5, sum_second, 0)
    sum_first(7, 0)
    lax.fori_loop(5, 8, sum_second, 0)

    for n in range(8):
        un = b * 2 + n // 4
        mine = diagonal & (un == u) & (n % 4 == v)

        @pl.when(jnp.logical_not(mine))
        def _():
            remote(sum2.at[0], result.at[pl.ds(n * 16, 16)], last_send.at[0], last_recv.at[n], sibling).wait_recv()

    out_ref[...] = result[...]

    @pl.when(jnp.logical_not(diagonal))
    def _():
        pair.wait_send()
        w_swap.wait_send()
        p1_sib(0, 0).wait_send()
        for p in range(CHUNKS):
            swap(p).wait_send()

    for i in (0, 1):
        for s in (1, 2, 3):
            p1_ring(i, s).wait_send()
            p1_sib(i, s).wait_send()
        p1_half(i).wait_send()
    p1_sib(0, 4).wait_send()

    def drain(p, carry):
        sib(p, 0, 0).wait_send()
        sib(p, 7, 4).wait_send()
        for i in (0, 1):
            for s in (1, 2, 3):
                ring(i, p, s).wait_send()
                sib_of(p, i, s).wait_send()

            @pl.when((p < 2) if i == 0 else (p >= 2))
            def _():
                ring(i, p, 4).wait_send()

        return carry

    lax.fori_loop(0, CHUNKS, drain, 0)

    def drain_sums(n, carry):
        for j in (1, 2, 3):
            first_copy(n, j).wait_send()
            second_copy(n, j).wait_send()

        @pl.when(jnp.logical_not(stays(n)))
        def _():
            last_copy(n).wait_send()

        return carry

    lax.fori_loop(0, NZ, drain_sums, 0)


def per_device(queries, compressed, kv_up, w_out, positions, latent_gain):
    bf16, f32 = jnp.bfloat16, jnp.float32
    dma = pltpu.SemaphoreType.DMA
    any_space = pl.BlockSpec(memory_space=pl.ANY)
    vmem = pl.BlockSpec(memory_space=pltpu.VMEM)
    return pl.pallas_call(
        kernel,
        out_shape=jax.ShapeDtypeStruct((ROWS, COLS), bf16),
        in_specs=[any_space, vmem, any_space, any_space, vmem, vmem],
        out_specs=vmem,
        scratch_shapes=[
            pltpu.VMEM((NZ * 2 * ROWS, WIDE), bf16),
            pltpu.VMEM((HEADS_DEV, ROWS, 256), bf16),
            pltpu.VMEM((ROWS, HEADS_DEV * QK), bf16),
            pltpu.VMEM((LAT, HEADS_DEV * 256), bf16),
            pltpu.VMEM((HEADS_DEV, VD, LAT), bf16),
            pltpu.VMEM((HEADS_DEV, NZ * 2 * ROWS, NOPE), bf16),
            pltpu.VMEM((HEADS_DEV, VD, NZ * 2 * ROWS), bf16),
            pltpu.VMEM((NZ * 2 * ROWS, ROWS), f32),
            pltpu.VMEM((CHUNKS, ROWS, 256), bf16),
            pltpu.VMEM((CHUNKS, NZ * 2 * ROWS, 256), bf16),
            pltpu.VMEM((HEADS_DEV * VD, COLS), bf16),
            pltpu.VMEM((NZ, 2 * ROWS, COLS), bf16),
            pltpu.VMEM((NZ, 3, 64, COLS), bf16),
            pltpu.VMEM((NZ, 64, COLS), bf16),
            pltpu.VMEM((NZ, 3, 16, COLS), bf16),
            pltpu.VMEM((NZ, 16, COLS), bf16),
            pltpu.VMEM((ROWS, COLS), bf16),
            dma((2, 4)), dma((2, 4)),
            dma((2, 5)), dma((2, 5)),
            dma, dma,
            dma, dma,
            dma((3,)),
            dma((2, CHUNKS, 4)), dma((2, CHUNKS, 4)),
            dma((CHUNKS, 8)), dma((CHUNKS, 8)),
            dma((CHUNKS,)), dma((CHUNKS,)),
            dma((NZ, 3)), dma((NZ, 3)),
            dma((NZ, 3)), dma((NZ, 3)),
            dma((NZ,)), dma((NZ,)),
        ],
        compiler_params=pltpu.CompilerParams(
            collective_id=0, has_side_effects=True, vmem_limit_bytes=56 * 1024 * 1024
        ),
        name="prefill",
    )(queries, compressed, kv_up, w_out, positions.reshape(1, ROWS), latent_gain.reshape(1, LAT))


def solution(mesh):
    in_specs = (P("ctx", "head"), P("ctx", None), P(None, "head"), P("head", "ctx"), P("ctx"), P())
    return jax.shard_map(
        per_device, mesh=mesh, in_specs=in_specs, out_specs=P("head", "ctx"), check_vma=False
    )
```

time: 334 us -> 99.2 us (0.30)
  the two profiles are of different devices: /device:TPU:6 before, /device:TPU:5 now
where the time goes in v1:
time: 99.2 us; the launch traced here: 99.1 us
  Pallas kernels  93.4 us (94%)
  local copies, waits for them, and re-layouts  5.64 us (6%)
    pallas_call x1, Pallas kernels, per_device(): pl.pallas_call(kernel, out_shape=jax.ShapeDtypeStruct((ROWS, COLS), bf16)...  93.4 us
    unnamed x2, local copies, waits for them, and re-layouts  3.97 us

profile of v1, /device:TPU:5, one launch (start us, length us, event | category | flops | bytes accessed | tf_op | source)
XLA Modules:
  0.0 99.1 jit_solution(7992139040280999752)
XLA Ops:
  0.0 1.7 %copy.7.comp_ref = bf16[128,576]{1,0:T(8,128)(2,1)} copy(bf16[128,576]{0,1:T(8,128)(2,1)} %param.7) | data formatting | bytes 294912 | tf_op args[1]
  1.7 2.3 %copy.8.w_hbm = bf16[1024,448]{1,0:T(8,128)(2,1)} copy(bf16[1024,448]{0,1:T(8,128)(2,1)} %param.9) | data formatting | bytes 1835008 | tf_op args[3]
  4.0 93.4 %prefill.1 = bf16[128,448]{1,0:T(8,128)(2,1)} custom-call(bf16[128,1536]{1,0:T(8,128)(2,1)} %q_hbm.1, bf16[128,576]{1,0:T(8,128)(2,1)} %copy.7.comp_ref, bf16[512,2048]{1,0:T(8,128)(2,1)} %kv_hbm.1, bf16[1024,448]{1,0:T(8,128)(2,1)} %copy.8.w_hbm, s32[1,128]{1,0:T(1,128)} %bitcast.3, f32[1,512]{1,0:T(1,128)} %bitcast.2), custom_call_target="tpu_custom_call" | custom-call | tf_op jit(solution)/shard_map/prefill/pallas_call | solution.py:451
  97.4 1.7 %copy.9 = bf16[128,448]{0,1:T(8,128)(2,1)} copy(bf16[128,448]{1,0:T(8,128)(2,1)} %prefill.1) | data formatting | bytes 229376 | tf_op jit(solution)/shard_map/prefill/pallas_call | solution.py:451

commit v2 on v1

v2 whole, which is shorter than its diff:
```python
import math

import jax
import jax.numpy as jnp
from jax import lax
from jax.experimental import pallas as pl
from jax.experimental.pallas import tpu as pltpu
from jax.sharding import PartitionSpec as P

LAT = 512
NOPE = 128
ROPE = 64
VD = 128
QK = 192
WIDE = 640
ROWS = 128
HEADS_DEV = 8
CHUNKS = 4
NZ = 8
COLS = 448
MESH = pl.DeviceIdType.MESH
SCALE = math.log2(math.e) / math.sqrt(QK)
NT = (((1,), (1,)), ((), ()))


def kernel(
    q_hbm, comp_ref, kv_hbm, w_hbm, pos_ref, gain_ref, out_ref,
    packed, qcat, q_in, kv_in, kv_t, stats, acc, att, full, w_buf, part, got1, sum1, got2, sum2, result,
    far_send, far_recv, near_send, near_recv, half_send, half_recv,
    w_send, w_recv, load_sem,
    ring_send, ring_recv, sib_send, sib_recv, swap_send, swap_recv,
    first_send, first_recv, second_send, second_recv, last_send, last_recv,
):
    ctx, head = lax.axis_index("ctx"), lax.axis_index("head")
    z, a = ctx // 2, ctx % 2
    xh, y, b = head // 8, (head // 2) % 4, head % 2
    x = xh * 2 + a
    diagonal = a == b
    partner = (z * 2 + b, xh * 8 + y * 2 + a)
    sibling = (ctx, xh * 8 + y * 2 + (1 - b))

    def along_z(d):
        return (((z + d + NZ) % NZ) * 2 + a, head)

    def partner_z(d):
        return (((z + d + NZ) % NZ) * 2 + b, xh * 8 + y * 2 + a)

    def in_plane(px, py, core):
        return (z * 2 + px % 2, (px // 2) * 8 + py * 2 + core)

    def block(dz, core):
        return ((z + dz + 2 * NZ) % NZ) * 2 + core

    def rows(blk):
        return pl.ds(pl.multiple_of(blk * ROWS, ROWS), ROWS)

    def remote(src, dst, send, recv, device):
        return pltpu.make_async_remote_copy(
            src_ref=src, dst_ref=dst, send_sem=send, recv_sem=recv, device_id=device, device_id_type=MESH
        )

    kv_load = pltpu.make_async_copy(kv_hbm, kv_in, load_sem.at[0])
    q_load = pltpu.make_async_copy(q_hbm, q_in, load_sem.at[1])
    kv_load.start()
    q_load.start()

    bar = pltpu.get_barrier_semaphore()

    def greet(k, carry):
        n = (a * 16 + head + k) % 32
        pl.semaphore_signal(bar, inc=1, device_id=(z * 2 + n // 16, n % 16), device_id_type=MESH)
        return carry

    lax.fori_loop(1, 32, greet, 0)
    for d in range(1, NZ):
        pl.semaphore_signal(bar, inc=1, device_id=along_z(d), device_id_type=MESH)
    for d in (1, -1):

        @pl.when(jnp.logical_not(diagonal))
        def _():
            pl.semaphore_signal(bar, inc=1, device_id=partner_z(d), device_id_type=MESH)

    latent = comp_ref[:LAT, :].astype(jnp.float32).T
    normed = latent * lax.rsqrt(jnp.mean(latent * latent, axis=-1, keepdims=True) + 1e-06) * gain_ref[...]
    own = rows(ctx)
    packed[own, :LAT] = normed.astype(jnp.bfloat16)
    pos = pos_ref[...]
    high = jnp.broadcast_to((pos >> 6).astype(jnp.float32), (ROWS, ROWS)).T
    low = jnp.broadcast_to((pos & 63).astype(jnp.float32), (ROWS, ROWS)).T
    lane = lax.broadcasted_iota(jnp.int32, (ROWS, ROWS), 1)
    rope = comp_ref[LAT:, :].astype(jnp.float32)
    rope = jnp.concatenate([rope, rope], axis=0).T
    tail = jnp.where(lane < 64, rope, jnp.where(lane < 96, high, low))
    packed[own, LAT:] = tail.astype(jnp.bfloat16)

    pl.semaphore_wait(bar, jnp.where(diagonal, 38, 40))

    def far(n):
        return (z + jnp.where(n % 2 == 1, -((n + 1) // 2), n // 2) + NZ) % NZ

    w_swap = remote(w_hbm, w_buf, w_send, w_recv, partner)
    w_load = pltpu.make_async_copy(w_hbm, w_buf, load_sem.at[2])

    def piece(n, col, first, count):
        start = (far(n) * 2 + col) * ROWS + b * 64 + first
        return packed.at[pl.ds(pl.multiple_of(start, 32), count)]

    def from_far(n):
        d = (n + 1) // 2 if n % 2 == 1 else -(n // 2)
        ref = piece(0, a, (y % 2) * 32, 32)
        return remote(ref, ref, far_send.at[n], far_recv.at[n], along_z(d))

    def from_near(k, n):
        ref = piece(n, a, (y % 2) * 32, 32)
        turn = 1 - 2 * b
        device = in_plane((x + 4 + turn * (k > 0)) % 4, (y + 4 + turn * (k != 1)) % 4, b)
        return remote(ref, ref, near_send.at[k, n], near_recv.at[k, n], device)

    def half(k, n):
        ref = piece(n, 1 - a if k else a, 0, 64)
        return remote(ref, ref, half_send.at[k, n], half_recv.at[k, n], sibling)

    def go(copies):
        for copy in copies:
            copy.start()

    def arrive(copies):
        for copy in copies:
            copy.wait_recv()

    go([from_far(n) for n in range(1, NZ)])
    go([from_near(1, 0), from_near(2, 0)])

    @pl.when(jnp.logical_not(diagonal))
    def _():
        w_swap.start()

    @pl.when(diagonal)
    def _():
        w_load.start()

    kv_load.wait()
    for h in range(HEADS_DEV):
        kv_t[h] = kv_in[:, h * 256 + NOPE : (h + 1) * 256].astype(jnp.float32).T.astype(jnp.bfloat16)
    q_load.wait()
    for j in range(HEADS_DEV // 2):
        first = q_in[:, j * 384 : j * 384 + 128]
        second = q_in[:, j * 384 + 128 : j * 384 + 256].astype(jnp.float32)
        third = q_in[:, j * 384 + 256 : j * 384 + 384].astype(jnp.float32)
        second_turned = pltpu.roll(second, 64, 1)
        third_turned = pltpu.roll(third, 64, 1)
        qcat[2 * j, :, :NOPE] = first
        qcat[2 * j, :, NOPE:] = jnp.where(lane < 64, second, 0.0).astype(jnp.bfloat16)
        qcat[2 * j + 1, :, :NOPE] = jnp.where(lane < 64, second_turned, third_turned).astype(jnp.bfloat16)
        qcat[2 * j + 1, :, NOPE:] = jnp.where(lane < 64, third_turned, 0.0).astype(jnp.bfloat16)

    for h in range(HEADS_DEV):
        stats[h, 0:1, :] = jnp.full((1, ROWS), -1e30, jnp.float32)
        stats[h, 1:2, :] = jnp.zeros((1, ROWS), jnp.float32)
        acc[h] = jnp.zeros((VD, ROWS), jnp.float32)

    def attend(blk0, blk1):
        both = jnp.concatenate([packed[rows(blk0), :LAT], packed[rows(blk1), :LAT]], axis=0)
        extra = jnp.concatenate([packed[rows(blk0), LAT:], packed[rows(blk1), LAT:]], axis=0)
        wide = extra.astype(jnp.float32)
        key_pos = wide[:, 64:65] * 64.0 + wide[:, 96:97]
        bias = jnp.where(key_pos <= pos.astype(jnp.float32), 0.0, -1e30)
        heads = range(HEADS_DEV)
        ks, vs = [], []
        for hp in range(HEADS_DEV // 2):
            k_cols = jnp.concatenate([kv_in[:, hp * 512 + i * 256 : hp * 512 + i * 256 + NOPE] for i in (0, 1)], axis=1)
            ks.append(jnp.dot(both, k_cols, preferred_element_type=jnp.float32).astype(jnp.bfloat16))
            v_rows = jnp.concatenate([kv_t[hp * 2], kv_t[hp * 2 + 1]], axis=0)
            vs.append(lax.dot_general(v_rows, both, NT, preferred_element_type=jnp.float32).astype(jnp.bfloat16))
        scores = []
        for h in heads:
            k_all = jnp.concatenate([ks[h // 2][:, h % 2 * 128 : h % 2 * 128 + 128], extra], axis=1)
            scores.append(lax.dot_general(k_all, qcat[h], NT, preferred_element_type=jnp.float32) * SCALE + bias)
        exps, fades = [], []
        for h in heads:
            before = stats[h, 0:1, :]
            top = jnp.maximum(before, jnp.max(scores[h], axis=0, keepdims=True))
            fade = jnp.exp2(before - top)
            e = jnp.exp2(scores[h] - top)
            stats[h, 0:1, :] = top
            stats[h, 1:2, :] = stats[h, 1:2, :] * fade + jnp.sum(e, axis=0, keepdims=True)
            exps.append(e.astype(jnp.bfloat16))
            fades.append(fade)
        for h in heads:
            v = vs[h // 2][h % 2 * 128 : h % 2 * 128 + 128, :]
            acc[h] = acc[h] * fades[h] + jnp.dot(v, exps[h], preferred_element_type=jnp.float32)

    def from_z(*ns):
        for n in ns:
            from_far(n).wait_recv()
            go([from_near(k, n) for k in range(3)])

    def from_plane(*ns):
        for n in ns:
            arrive([from_near(k, n) for k in range(3)])
            go([half(k, n) for k in (0, 1)])

    def before_stage(g):
        if g == 0:
            arrive([from_near(1, 0), from_near(2, 0)])
            half(1, 0).start()
            from_z(1, 2)
            half(1, 0).wait_recv()
        if g == 1:
            from_z(3, 4)
            from_plane(1, 2)
        if g == 2:
            from_z(5, 6)
        if g == 3:
            from_z(7)
            from_plane(3, 4)
        if g == 4:
            from_plane(5)
        if g == 5:
            from_plane(6, 7)
        if g > 0:
            arrive([half(k, g) for k in (0, 1)])

    def stage(g, carry):
        for k in range(NZ):
            @pl.when(g == k)
            def _():
                before_stage(k)

        attend(far(g) * 2, far(g) * 2 + 1)
        return carry

    lax.fori_loop(0, NZ, stage, 0)

    def ring(i, p, s):
        d = 1 if i == 0 else -1
        r = rows(block(-d * (s - 1), b))
        return remote(full.at[p, r], full.at[p, r], ring_send.at[i, p, s - 1], ring_recv.at[i, p, s - 1], along_z(d))

    def sib(p, n, dz):
        r = rows(block(dz, b))
        return remote(full.at[p, r], full.at[p, r], sib_send.at[p, n], sib_recv.at[p, n], sibling)

    def swap(p):
        return remote(att.at[p], full.at[p, own], swap_send.at[p], swap_recv.at[p], partner)

    def sib_of(p, i, s):
        d = 1 if i == 0 else -1
        return sib(p, i * 3 + s, -d * s)

    def ring_first(i, p):
        return remote(
            att.at[p], full.at[p, own], ring_send.at[i, p, 0], ring_recv.at[i, p, 0], partner_z(1 if i == 0 else -1)
        )

    def pass_on(p, s):
        if s < 4:
            for i in (0, 1):
                ring(i, p, s).wait_recv()
                if s < 3 or i == p // 2:
                    ring(i, p, s + 1).start()
                sib_of(p, i, s).start()
        else:
            ring(p // 2, p, 4).wait_recv()
            sib(p, 7, 4).start()

    for p in range(CHUNKS):
        for i in (0, 1):
            o = acc[2 * p + i] / stats[2 * p + i, 1:2, :]
            att[p, :, i * VD : (i + 1) * VD] = o.T.astype(jnp.bfloat16)
        ring_first(0, p).start()
        ring_first(1, p).start()

        @pl.when(diagonal)
        def _():
            full[p, own, :] = att[p]
            sib(p, 0, 0).start()

        @pl.when(jnp.logical_not(diagonal))
        def _():
            swap(p).start()

    def home(chunks):
        @pl.when(jnp.logical_not(diagonal))
        def _():
            for p in chunks:
                swap(p).wait_recv()
                sib(p, 0, 0).start()

    pass_on(0, 1)
    pass_on(1, 1)
    home((0, 1, 2, 3))

    u = jnp.where(b == 0, y, x)
    v = jnp.where(b == 0, x, y)

    def first_copy(n, j):
        t = (u + j) % 4
        device = in_plane(jnp.where(b == 0, x, t), jnp.where(b == 0, t, y), b)
        src = part.at[n, pl.ds(pl.multiple_of(t * 64, 64), 64)]
        return remote(src, got1.at[n, j - 1], first_send.at[n, j - 1], first_recv.at[n, j - 1], device)

    def second_copy(n, j):
        t = (v + j) % 4
        device = in_plane(jnp.where(b == 0, t, x), jnp.where(b == 0, y, t), b)
        src = sum1.at[n, pl.ds(pl.multiple_of(t * 16, 16), 16)]
        return remote(src, got2.at[n, j - 1], second_send.at[n, j - 1], second_recv.at[n, j - 1], device)

    def project(n, carry):
        zp = far(n)
        for i in (0, 1):
            r = rows(zp * 2 + i)
            lhs = jnp.concatenate([full[p, r, :] for p in range(CHUNKS)], axis=1)
            part[n, i * ROWS : (i + 1) * ROWS, :] = lax.dot_general(
                lhs, w_buf[...], NT, preferred_element_type=jnp.float32
            ).astype(jnp.bfloat16)
        for j in (1, 2, 3):
            first_copy(n, j).start()
        return carry

    def sum_first(n, carry):
        total = part[n, pl.ds(pl.multiple_of(u * 64, 64), 64), :].astype(jnp.float32)
        for j in (1, 2, 3):
            first_copy(n, j).wait_recv()
        for j in (1, 2, 3):
            total = total + got1[n, j - 1].astype(jnp.float32)
        sum1[n] = total.astype(jnp.bfloat16)
        for j in (1, 2, 3):
            second_copy(n, j).start()
        return carry

    slot = (u % 2) * 4 + v

    def last_copy(n):
        zp = far(n)
        device = in_plane((zp // 4) * 2 + b, zp % 4, u // 2)
        return remote(
            sum2.at[n], result.at[pl.ds(pl.multiple_of(slot * 16, 16), 16)], last_send.at[n], last_recv.at[slot], device
        )

    def stays(n):
        zp = far(n)
        return diagonal & (u // 2 == b) & (zp == xh * 4 + y)

    def sum_second(n, carry):
        total = sum1[n, pl.ds(pl.multiple_of(v * 16, 16), 16), :].astype(jnp.float32)
        for j in (1, 2, 3):
            second_copy(n, j).wait_recv()
        for j in (1, 2, 3):
            total = total + got2[n, j - 1].astype(jnp.float32)
        sum2[n] = total.astype(jnp.bfloat16)

        @pl.when(stays(n))
        def _():
            result[pl.ds(pl.multiple_of(slot * 16, 16), 16), :] = sum2[n]

        @pl.when(jnp.logical_not(stays(n)))
        def _():
            last_copy(n).start()

        return carry

    def sib_wait(i, s):
        for p in range(CHUNKS):
            sib_of(p, i, s).wait_recv()

    @pl.when(diagonal)
    def _():
        w_load.wait()

    @pl.when(jnp.logical_not(diagonal))
    def _():
        w_swap.wait_recv()

    def project_round(s):
        for i in (0, 1):
            sib_wait(i, s)
        lax.fori_loop(2 * s - 1, 2 * s + 1, project, 0)

    for p in (2, 3):
        pass_on(p, 1)
    for p in range(CHUNKS):
        sib(p, 0, 0).wait_recv()
    project(0, 0)
    pass_on(0, 2)
    pass_on(1, 2)
    project_round(1)
    pass_on(2, 2)
    pass_on(3, 2)
    pass_on(0, 3)
    pass_on(1, 3)
    project_round(2)
    pass_on(2, 3)
    pass_on(3, 3)
    lax.fori_loop(0, 3, sum_first, 0)
    pass_on(0, 4)
    pass_on(2, 4)
    project_round(3)
    pass_on(1, 4)
    pass_on(3, 4)
    lax.fori_loop(3, 5, sum_first, 0)
    lax.fori_loop(0, 3, sum_second, 0)
    for p in range(CHUNKS):
        sib(p, 7, 4).wait_recv()
    project(7, 0)
    lax.fori_loop(5, 7, sum_first, 0)
    lax.fori_loop(3, 5, sum_second, 0)
    sum_first(7, 0)
    lax.fori_loop(5, 8, sum_second, 0)

    for n in range(8):
        un = b * 2 + n // 4
        mine = diagonal & (un == u) & (n % 4 == v)

        @pl.when(jnp.logical_not(mine))
        def _():
            remote(sum2.at[0], result.at[pl.ds(n * 16, 16)], last_send.at[0], last_recv.at[n], sibling).wait_recv()

    out_ref[...] = result[...].astype(jnp.float32).T.astype(jnp.bfloat16)

    @pl.when(jnp.logical_not(diagonal))
    def _():
        w_swap.wait_send()
        for p in range(CHUNKS):
            swap(p).wait_send()

    for n in range(NZ):
        for k in range(3):
            if n > 0 or k > 0:
                from_near(k, n).wait_send()
        for k in (0, 1):
            if n > 0 or k > 0:
                half(k, n).wait_send()
        if n > 0:
            from_far(n).wait_send()

    def drain(p, carry):
        sib(p, 0, 0).wait_send()
        sib(p, 7, 4).wait_send()
        for i in (0, 1):
            for s in (1, 2, 3):
                sib_of(p, i, s).wait_send()
            for s in (2, 3):
                ring(i, p, s).wait_send()

            ring(i, p, 1).wait_send()

            @pl.when((p < 2) if i == 0 else (p >= 2))
            def _():
                ring(i, p, 4).wait_send()

        return carry

    lax.fori_loop(0, CHUNKS, drain, 0)

    def drain_sums(n, carry):
        for j in (1, 2, 3):
            first_copy(n, j).wait_send()
            second_copy(n, j).wait_send()

        @pl.when(jnp.logical_not(stays(n)))
        def _():
            last_copy(n).wait_send()

        return carry

    lax.fori_loop(0, NZ, drain_sums, 0)


def per_device(queries, compressed, kv_up, w_out, positions, latent_gain):
    bf16, f32 = jnp.bfloat16, jnp.float32
    dma = pltpu.SemaphoreType.DMA
    any_space = pl.BlockSpec(memory_space=pl.ANY)
    vmem = pl.BlockSpec(memory_space=pltpu.VMEM)
    return pl.pallas_call(
        kernel,
        out_shape=jax.ShapeDtypeStruct((COLS, ROWS), bf16),
        in_specs=[any_space, vmem, any_space, any_space, vmem, vmem],
        out_specs=vmem,
        scratch_shapes=[
            pltpu.VMEM((NZ * 2 * ROWS, WIDE), bf16),
            pltpu.VMEM((HEADS_DEV, ROWS, 256), bf16),
            pltpu.VMEM((ROWS, HEADS_DEV * QK), bf16),
            pltpu.VMEM((LAT, HEADS_DEV * 256), bf16),
            pltpu.VMEM((HEADS_DEV, VD, LAT), bf16),
            pltpu.VMEM((HEADS_DEV, 8, ROWS), f32),
            pltpu.VMEM((HEADS_DEV, VD, ROWS), f32),
            pltpu.VMEM((CHUNKS, ROWS, 256), bf16),
            pltpu.VMEM((CHUNKS, NZ * 2 * ROWS, 256), bf16),
            pltpu.VMEM((COLS, HEADS_DEV * VD), bf16),
            pltpu.VMEM((NZ, 2 * ROWS, COLS), bf16),
            pltpu.VMEM((NZ, 3, 64, COLS), bf16),
            pltpu.VMEM((NZ, 64, COLS), bf16),
            pltpu.VMEM((NZ, 3, 16, COLS), bf16),
            pltpu.VMEM((NZ, 16, COLS), bf16),
            pltpu.VMEM((ROWS, COLS), bf16),
            dma((NZ,)), dma((NZ,)),
            dma((3, NZ)), dma((3, NZ)),
            dma((2, NZ)), dma((2, NZ)),
            dma, dma,
            dma((3,)),
            dma((2, CHUNKS, 4)), dma((2, CHUNKS, 4)),
            dma((CHUNKS, 8)), dma((CHUNKS, 8)),
            dma((CHUNKS,)), dma((CHUNKS,)),
            dma((NZ, 3)), dma((NZ, 3)),
            dma((NZ, 3)), dma((NZ, 3)),
            dma((NZ,)), dma((NZ,)),
        ],
        compiler_params=pltpu.CompilerParams(
            collective_id=0, has_side_effects=True, vmem_limit_bytes=56 * 1024 * 1024
        ),
        name="prefill",
    )(queries, compressed.T, kv_up, w_out.T, positions.reshape(1, ROWS), latent_gain.reshape(1, LAT)).T


def solution(mesh):
    in_specs = (P("ctx", "head"), P("ctx", None), P(None, "head"), P("head", "ctx"), P("ctx"), P())
    return jax.shard_map(
        per_device, mesh=mesh, in_specs=in_specs, out_specs=P("head", "ctx"), check_vma=False
    )
```

time: 99.2 us -> 80.9 us (0.82)
  Pallas kernels: 93.4 us -> 79.2 us
  local copies, waits for them, and re-layouts: 5.64 us -> 1.55 us
    pallas_call x1, Pallas kernels: 93.4 us -> 79.2 us  [per_device(): pl.pallas_call(kernel, out_shape=jax.ShapeDtypeStruct((COLS, ROWS), bf16)...]
    unnamed x2 -> x1, local copies, waits for them, and re-layouts: 3.97 us -> 1.55 us
    pallas_call x1 -> x0, local copies, waits for them, and re-layouts: 1.67 us -> none  [per_device(): pl.pallas_call(kernel, out_shape=jax.ShapeDtypeStruct((ROWS, COLS), bf16)...]
where the time goes in v2:
time: 80.9 us; the launch traced here: 80.8 us
  Pallas kernels  79.2 us (98%)
  local copies, waits for them, and re-layouts  1.55 us (2%)
    pallas_call x1, Pallas kernels, per_device(): pl.pallas_call(kernel, out_shape=jax.ShapeDtypeStruct((COLS, ROWS), bf16)...  79.2 us

profile of v2, /device:TPU:5, one launch (start us, length us, event | category | flops | bytes accessed | tf_op | source)
XLA Modules:
  0.0 80.8 jit_solution(8362340475003241648)
XLA Ops:
  0.0 79.2 %prefill.1 = bf16[448,128]{1,0:T(8,128)(2,1)} custom-call(bf16[128,1536]{1,0:T(8,128)(2,1)} %q_hbm.1, bf16[576,128]{1,0:T(8,128)(2,1)} %bitcast.7, bf16[512,2048]{1,0:T(8,128)(2,1)} %kv_hbm.1, bf16[448,1024]{1,0:T(8,128)(2,1)} %bitcast.5, s32[1,128]{1,0:T(1,128)} %bitcast.9, f32[1,512]{1,0:T(1,128)} %bitcast.8), custom_call_target="tpu_custom_call" | custom-call | tf_op jit(solution)/shard_map/prefill/pallas_call | solution.py:475
  79.2 1.6 %copy.8 = bf16[128,448]{0,1:T(8,128)(2,1)} copy(bf16[128,448]{0,1:T(8,128)(2,1)} %bitcast.6) | data formatting | bytes 229376

commit v3 on v2

--- a/solution.py
+++ b/solution.py
@@ -25,10 +25,10 @@
 
 def kernel(
     q_hbm, comp_ref, kv_hbm, w_hbm, pos_ref, gain_ref, out_ref,
-    packed, qcat, q_in, kv_in, kv_t, stats, acc, att, full, w_buf, part, got1, sum1, got2, sum2, result,
+    packed, qcat, q_in, kv_in, kv_t, stats, acc, att, full, w_both, part, got1, sum1, got2, sum2, result,
     far_send, far_recv, near_send, near_recv, half_send, half_recv,
-    w_send, w_recv, load_sem,
-    ring_send, ring_recv, sib_send, sib_recv, swap_send, swap_recv,
+    w_send, w_recv, w2_send, w2_recv, load_sem,
+    ring_send, ring_recv, swap_send, swap_recv,
     first_send, first_recv, second_send, second_recv, last_send, last_recv,
 ):
     ctx, head = lax.axis_index("ctx"), lax.axis_index("head")
@@ -67,11 +67,18 @@
     bar = pltpu.get_barrier_semaphore()
 
     def greet(k, carry):
-        n = (a * 16 + head + k) % 32
-        pl.semaphore_signal(bar, inc=1, device_id=(z * 2 + n // 16, n % 16), device_id_type=MESH)
-        return carry
-
-    lax.fori_loop(1, 32, greet, 0)
+        pl.semaphore_signal(
+            bar, inc=1, device_id=in_plane((x + k // 4) % 4, (y + k % 4) % 4, b), device_id_type=MESH
+        )
+        return carry
+
+    lax.fori_loop(1, 16, greet, 0)
+    pl.semaphore_signal(bar, inc=1, device_id=sibling, device_id_type=MESH)
+
+    @pl.when(jnp.logical_not(diagonal))
+    def _():
+        pl.semaphore_signal(bar, inc=1, device_id=partner, device_id_type=MESH)
+
     for d in range(1, NZ):
         pl.semaphore_signal(bar, inc=1, device_id=along_z(d), device_id_type=MESH)
     for d in (1, -1):
@@ -93,13 +100,14 @@
     tail = jnp.where(lane < 64, rope, jnp.where(lane < 96, high, low))
     packed[own, LAT:] = tail.astype(jnp.bfloat16)
 
-    pl.semaphore_wait(bar, jnp.where(diagonal, 38, 40))
+    pl.semaphore_wait(bar, jnp.where(diagonal, 23, 26))
 
     def far(n):
         return (z + jnp.where(n % 2 == 1, -((n + 1) // 2), n // 2) + NZ) % NZ
 
-    w_swap = remote(w_hbm, w_buf, w_send, w_recv, partner)
-    w_load = pltpu.make_async_copy(w_hbm, w_buf, load_sem.at[2])
+    w_swap = remote(w_hbm, w_both.at[a], w_send, w_recv, partner)
+    w_load = pltpu.make_async_copy(w_hbm, w_both.at[b], load_sem.at[2])
+    w_share = remote(w_both.at[b], w_both.at[b], w2_send, w2_recv, sibling)
 
     def piece(n, col, first, count):
         start = (far(n) * 2 + col) * ROWS + b * 64 + first
@@ -107,7 +115,10 @@
 
     def from_far(n):
         d = (n + 1) // 2 if n % 2 == 1 else -(n // 2)
-        ref = piece(0, a, (y % 2) * 32, 32)
+        hop = n in (5, 6)
+        if hop:
+            d = 1 if n == 5 else -1
+        ref = piece(n - 2 if hop else 0, a, (y % 2) * 32, 32)
         return remote(ref, ref, far_send.at[n], far_recv.at[n], along_z(d))
 
     def from_near(k, n):
@@ -128,7 +139,7 @@
         for copy in copies:
             copy.wait_recv()
 
-    go([from_far(n) for n in range(1, NZ)])
+    go([from_far(n) for n in (1, 2, 3, 4, 7)])
     go([from_near(1, 0), from_near(2, 0)])
 
     @pl.when(jnp.logical_not(diagonal))
@@ -159,24 +170,23 @@
         stats[h, 1:2, :] = jnp.zeros((1, ROWS), jnp.float32)
         acc[h] = jnp.zeros((VD, ROWS), jnp.float32)
 
-    def attend(blk0, blk1):
+    def attend(blk0, blk1, pairs):
         both = jnp.concatenate([packed[rows(blk0), :LAT], packed[rows(blk1), :LAT]], axis=0)
         extra = jnp.concatenate([packed[rows(blk0), LAT:], packed[rows(blk1), LAT:]], axis=0)
         wide = extra.astype(jnp.float32)
         key_pos = wide[:, 64:65] * 64.0 + wide[:, 96:97]
         bias = jnp.where(key_pos <= pos.astype(jnp.float32), 0.0, -1e30)
-        heads = range(HEADS_DEV)
-        ks, vs = [], []
-        for hp in range(HEADS_DEV // 2):
+        heads = [2 * hp + i for hp in pairs for i in (0, 1)]
+        ks, vs = {}, {}
+        for hp in pairs:
             k_cols = jnp.concatenate([kv_in[:, hp * 512 + i * 256 : hp * 512 + i * 256 + NOPE] for i in (0, 1)], axis=1)
-            ks.append(jnp.dot(both, k_cols, preferred_element_type=jnp.float32).astype(jnp.bfloat16))
+            ks[hp] = jnp.dot(both, k_cols, preferred_element_type=jnp.float32).astype(jnp.bfloat16)
             v_rows = jnp.concatenate([kv_t[hp * 2], kv_t[hp * 2 + 1]], axis=0)
-            vs.append(lax.dot_general(v_rows, both, NT, preferred_element_type=jnp.float32).astype(jnp.bfloat16))
-        scores = []
+            vs[hp] = lax.dot_general(v_rows, both, NT, preferred_element_type=jnp.float32).astype(jnp.bfloat16)
+        scores, exps, fades = {}, {}, {}
         for h in heads:
             k_all = jnp.concatenate([ks[h // 2][:, h % 2 * 128 : h % 2 * 128 + 128], extra], axis=1)
-            scores.append(lax.dot_general(k_all, qcat[h], NT, preferred_element_type=jnp.float32) * SCALE + bias)
-        exps, fades = [], []
+            scores[h] = lax.dot_general(k_all, qcat[h], NT, preferred_element_type=jnp.float32) * SCALE + bias
         for h in heads:
             before = stats[h, 0:1, :]
             top = jnp.maximum(before, jnp.max(scores[h], axis=0, keepdims=True))
@@ -184,8 +194,8 @@
             e = jnp.exp2(scores[h] - top)
             stats[h, 0:1, :] = top
             stats[h, 1:2, :] = stats[h, 1:2, :] * fade + jnp.sum(e, axis=0, keepdims=True)
-            exps.append(e.astype(jnp.bfloat16))
-            fades.append(fade)
+            exps[h] = e.astype(jnp.bfloat16)
+            fades[h] = fade
         for h in heads:
             v = vs[h // 2][h % 2 * 128 : h % 2 * 128 + 128, :]
             acc[h] = acc[h] * fades[h] + jnp.dot(v, exps[h], preferred_element_type=jnp.float32)
@@ -193,6 +203,8 @@
     def from_z(*ns):
         for n in ns:
             from_far(n).wait_recv()
+            if n in (3, 4):
+                from_far(n + 2).start()
             go([from_near(k, n) for k in range(3)])
 
     def from_plane(*ns):
@@ -217,36 +229,31 @@
         if g == 4:
             from_plane(5)
         if g == 5:
-            from_plane(6, 7)
+            from_plane(6)
+        if g == 6:
+            from_plane(7)
         if g > 0:
             arrive([half(k, g) for k in (0, 1)])
 
     def stage(g, carry):
-        for k in range(NZ):
+        for k in range(NZ - 1):
             @pl.when(g == k)
             def _():
                 before_stage(k)
 
-        attend(far(g) * 2, far(g) * 2 + 1)
-        return carry
-
-    lax.fori_loop(0, NZ, stage, 0)
+        attend(far(g) * 2, far(g) * 2 + 1, range(HEADS_DEV // 2))
+        return carry
+
+    lax.fori_loop(0, NZ - 1, stage, 0)
+    before_stage(NZ - 1)
 
     def ring(i, p, s):
         d = 1 if i == 0 else -1
         r = rows(block(-d * (s - 1), b))
         return remote(full.at[p, r], full.at[p, r], ring_send.at[i, p, s - 1], ring_recv.at[i, p, s - 1], along_z(d))
 
-    def sib(p, n, dz):
-        r = rows(block(dz, b))
-        return remote(full.at[p, r], full.at[p, r], sib_send.at[p, n], sib_recv.at[p, n], sibling)
-
     def swap(p):
         return remote(att.at[p], full.at[p, own], swap_send.at[p], swap_recv.at[p], partner)
-
-    def sib_of(p, i, s):
-        d = 1 if i == 0 else -1
-        return sib(p, i * 3 + s, -d * s)
 
     def ring_first(i, p):
         return remote(
@@ -259,12 +266,12 @@
                 ring(i, p, s).wait_recv()
                 if s < 3 or i == p // 2:
                     ring(i, p, s + 1).start()
-                sib_of(p, i, s).start()
         else:
             ring(p // 2, p, 4).wait_recv()
-            sib(p, 7, 4).start()
 
     for p in range(CHUNKS):
+        if p % 2 == 0:
+            attend(far(NZ - 1) * 2, far(NZ - 1) * 2 + 1, (p, p + 1))
         for i in (0, 1):
             o = acc[2 * p + i] / stats[2 * p + i, 1:2, :]
             att[p, :, i * VD : (i + 1) * VD] = o.T.astype(jnp.bfloat16)
@@ -274,22 +281,27 @@
         @pl.when(diagonal)
         def _():
             full[p, own, :] = att[p]
-            sib(p, 0, 0).start()
 
         @pl.when(jnp.logical_not(diagonal))
         def _():
             swap(p).start()
 
-    def home(chunks):
-        @pl.when(jnp.logical_not(diagonal))
-        def _():
-            for p in chunks:
-                swap(p).wait_recv()
-                sib(p, 0, 0).start()
-
+    @pl.when(diagonal)
+    def _():
+        w_load.wait()
+
+    @pl.when(jnp.logical_not(diagonal))
+    def _():
+        w_swap.wait_recv()
+
+    w_share.start()
     pass_on(0, 1)
     pass_on(1, 1)
-    home((0, 1, 2, 3))
+
+    @pl.when(jnp.logical_not(diagonal))
+    def _():
+        for p in range(CHUNKS):
+            swap(p).wait_recv()
 
     u = jnp.where(b == 0, y, x)
     v = jnp.where(b == 0, x, y)
@@ -307,12 +319,11 @@
         return remote(src, got2.at[n, j - 1], second_send.at[n, j - 1], second_recv.at[n, j - 1], device)
 
     def project(n, carry):
-        zp = far(n)
+        r = rows(far(n) * 2 + b)
+        lhs = jnp.concatenate([full[p, r, :] for p in range(CHUNKS)], axis=1)
         for i in (0, 1):
-            r = rows(zp * 2 + i)
-            lhs = jnp.concatenate([full[p, r, :] for p in range(CHUNKS)], axis=1)
             part[n, i * ROWS : (i + 1) * ROWS, :] = lax.dot_general(
-                lhs, w_buf[...], NT, preferred_element_type=jnp.float32
+                lhs, w_both[i], NT, preferred_element_type=jnp.float32
             ).astype(jnp.bfloat16)
         for j in (1, 2, 3):
             first_copy(n, j).start()
@@ -333,14 +344,14 @@
 
     def last_copy(n):
         zp = far(n)
-        device = in_plane((zp // 4) * 2 + b, zp % 4, u // 2)
+        device = in_plane((zp // 4) * 2 + u // 2, zp % 4, b)
         return remote(
             sum2.at[n], result.at[pl.ds(pl.multiple_of(slot * 16, 16), 16)], last_send.at[n], last_recv.at[slot], device
         )
 
     def stays(n):
         zp = far(n)
-        return diagonal & (u // 2 == b) & (zp == xh * 4 + y)
+        return (u // 2 == a) & (zp == xh * 4 + y)
 
     def sum_second(n, carry):
         total = sum1[n, pl.ds(pl.multiple_of(v * 16, 16), 16), :].astype(jnp.float32)
@@ -360,28 +371,30 @@
 
         return carry
 
-    def sib_wait(i, s):
-        for p in range(CHUNKS):
-            sib_of(p, i, s).wait_recv()
-
-    @pl.when(diagonal)
-    def _():
-        w_load.wait()
-
-    @pl.when(jnp.logical_not(diagonal))
-    def _():
-        w_swap.wait_recv()
-
     def project_round(s):
-        for i in (0, 1):
-            sib_wait(i, s)
         lax.fori_loop(2 * s - 1, 2 * s + 1, project, 0)
 
     for p in (2, 3):
         pass_on(p, 1)
-    for p in range(CHUNKS):
-        sib(p, 0, 0).wait_recv()
+    w_share.wait_recv()
     project(0, 0)
+
+    for n in range(NZ):
+        for k in range(3):
+            if n > 0 or k > 0:
+                from_near(k, n).wait_send()
+        for k in (0, 1):
+            if n > 0 or k > 0:
+                half(k, n).wait_send()
+        if n > 0:
+            from_far(n).wait_send()
+
+    @pl.when(jnp.logical_not(diagonal))
+    def _():
+        w_swap.wait_send()
+        for p in range(CHUNKS):
+            swap(p).wait_send()
+
     pass_on(0, 2)
     pass_on(1, 2)
     project_round(1)
@@ -400,17 +413,34 @@
     pass_on(3, 4)
     lax.fori_loop(3, 5, sum_first, 0)
     lax.fori_loop(0, 3, sum_second, 0)
+    project(7, 0)
+    w_share.wait_send()
     for p in range(CHUNKS):
-        sib(p, 7, 4).wait_recv()
-    project(7, 0)
+        for i in (0, 1):
+            for s in (1, 2, 3):
+                ring(i, p, s).wait_send()
+        ring(p // 2, p, 4).wait_send()
     lax.fori_loop(5, 7, sum_first, 0)
     lax.fori_loop(3, 5, sum_second, 0)
     sum_first(7, 0)
+
+    def first_left(n, carry):
+        for j in (1, 2, 3):
+            first_copy(n, j).wait_send()
+        return carry
+
+    def second_left(n, carry):
+        for j in (1, 2, 3):
+            second_copy(n, j).wait_send()
+        return carry
+
+    lax.fori_loop(0, NZ, first_left, 0)
     lax.fori_loop(5, 8, sum_second, 0)
+    lax.fori_loop(0, NZ, second_left, 0)
 
     for n in range(8):
-        un = b * 2 + n // 4
-        mine = diagonal & (un == u) & (n % 4 == v)
+        un = a * 2 + n // 4
+        mine = (un == u) & (n % 4 == v)
 
         @pl.when(jnp.logical_not(mine))
         def _():
@@ -418,53 +448,10 @@
 
     out_ref[...] = result[...].astype(jnp.float32).T.astype(jnp.bfloat16)
 
-    @pl.when(jnp.logical_not(diagonal))
-    def _():
-        w_swap.wait_send()
-        for p in range(CHUNKS):
-            swap(p).wait_send()
-
     for n in range(NZ):
-        for k in range(3):
-            if n > 0 or k > 0:
-                from_near(k, n).wait_send()
-        for k in (0, 1):
-            if n > 0 or k > 0:
-                half(k, n).wait_send()
-        if n > 0:
-            from_far(n).wait_send()
-
-    def drain(p, carry):
-        sib(p, 0, 0).wait_send()
-        sib(p, 7, 4).wait_send()
-        for i in (0, 1):
-            for s in (1, 2, 3):
-                sib_of(p, i, s).wait_send()
-            for s in (2, 3):
-                ring(i, p, s).wait_send()
-
-            ring(i, p, 1).wait_send()
-
-            @pl.when((p < 2) if i == 0 else (p >= 2))
-            def _():
-                ring(i, p, 4).wait_send()
-
-        return carry
-
-    lax.fori_loop(0, CHUNKS, drain, 0)
-
-    def drain_sums(n, carry):
-        for j in (1, 2, 3):
-            first_copy(n, j).wait_send()
-            second_copy(n, j).wait_send()
-
         @pl.when(jnp.logical_not(stays(n)))
         def _():
             last_copy(n).wait_send()
-
-        return carry
-
-    lax.fori_loop(0, NZ, drain_sums, 0)
 
 
 def per_device(queries, compressed, kv_up, w_out, positions, latent_gain):
@@ -487,7 +474,7 @@
             pltpu.VMEM((HEADS_DEV, VD, ROWS), f32),
             pltpu.VMEM((CHUNKS, ROWS, 256), bf16),
             pltpu.VMEM((CHUNKS, NZ * 2 * ROWS, 256), bf16),
-            pltpu.VMEM((COLS, HEADS_DEV * VD), bf16),
+            pltpu.VMEM((2, COLS, HEADS_DEV * VD), bf16),
             pltpu.VMEM((NZ, 2 * ROWS, COLS), bf16),
             pltpu.VMEM((NZ, 3, 64, COLS), bf16),
             pltpu.VMEM((NZ, 64, COLS), bf16),
@@ -498,9 +485,9 @@
             dma((3, NZ)), dma((3, NZ)),
             dma((2, NZ)), dma((2, NZ)),
             dma, dma,
+            dma, dma,
             dma((3,)),
             dma((2, CHUNKS, 4)), dma((2, CHUNKS, 4)),
-            dma((CHUNKS, 8)), dma((CHUNKS, 8)),
             dma((CHUNKS,)), dma((CHUNKS,)),
             dma((NZ, 3)), dma((NZ, 3)),
             dma((NZ, 3)), dma((NZ, 3)),

time: 80.9 us -> 77.2 us (0.954)
  the two profiles are of different devices: /device:TPU:5 before, /device:TPU:6 now
where the time goes in v3:
time: 77.2 us; the launch traced here: 77 us
  Pallas kernels  75.5 us (98%)
  local copies, waits for them, and re-layouts  1.55 us (2%)
    pallas_call x1, Pallas kernels, per_device(): pl.pallas_call(kernel, out_shape=jax.ShapeDtypeStruct((COLS, ROWS), bf16)...  75.5 us
    unnamed x1, local copies, waits for them, and re-layouts  1.55 us

profile of v3, /device:TPU:6, one launch (start us, length us, event | category | flops | bytes accessed | tf_op | source)
XLA Modules:
  0.0 77.0 jit_solution(6962576276241599699)
XLA Ops:
  0.0 75.5 %prefill.1 = bf16[448,128]{1,0:T(8,128)(2,1)} custom-call(bf16[128,1536]{1,0:T(8,128)(2,1)} %q_hbm.1, bf16[576,128]{1,0:T(8,128)(2,1)} %bitcast.7, bf16[512,2048]{1,0:T(8,128)(2,1)} %kv_hbm.1, bf16[448,1024]{1,0:T(8,128)(2,1)} %bitcast.5, s32[1,128]{1,0:T(1,128)} %bitcast.9, f32[1,512]{1,0:T(1,128)} %bitcast.8), custom_call_target="tpu_custom_call" | custom-call | tf_op jit(solution)/shard_map/prefill/pallas_call | solution.py:462
  75.5 1.6 %copy.8 = bf16[128,448]{0,1:T(8,128)(2,1)} copy(bf16[128,448]{0,1:T(8,128)(2,1)} %bitcast.6) | data formatting | bytes 229376

commit v4 on v3

--- a/solution.py
+++ b/solution.py
@@ -24,8 +24,8 @@
 
 
 def kernel(
-    q_hbm, comp_ref, kv_hbm, w_hbm, pos_ref, gain_ref, out_ref,
-    packed, qcat, q_in, kv_in, kv_t, stats, acc, att, full, w_both, part, got1, sum1, got2, sum2, result,
+    q_hbm, comp_hbm, kv_hbm, w_hbm, pos_hbm, gain_hbm, out_ref,
+    comp_ref, pos_ref, gain_ref, packed, qcat, q_in, kv_in, kv_t, stats, acc, att, full, w_both, part, got1, sum1, got2, sum2, result,
     far_send, far_recv, near_send, near_recv, half_send, half_recv,
     w_send, w_recv, w2_send, w2_recv, load_sem,
     ring_send, ring_recv, swap_send, swap_recv,
@@ -61,6 +61,12 @@
 
     kv_load = pltpu.make_async_copy(kv_hbm, kv_in, load_sem.at[0])
     q_load = pltpu.make_async_copy(q_hbm, q_in, load_sem.at[1])
+    small = [
+        pltpu.make_async_copy(src, dst, load_sem.at[3 + i])
+        for i, (src, dst) in enumerate([(comp_hbm, comp_ref), (pos_hbm, pos_ref), (gain_hbm, gain_ref)])
+    ]
+    for load in small:
+        load.start()
     kv_load.start()
     q_load.start()
 
@@ -72,13 +78,6 @@
         )
         return carry
 
-    lax.fori_loop(1, 16, greet, 0)
-    pl.semaphore_signal(bar, inc=1, device_id=sibling, device_id_type=MESH)
-
-    @pl.when(jnp.logical_not(diagonal))
-    def _():
-        pl.semaphore_signal(bar, inc=1, device_id=partner, device_id_type=MESH)
-
     for d in range(1, NZ):
         pl.semaphore_signal(bar, inc=1, device_id=along_z(d), device_id_type=MESH)
     for d in (1, -1):
@@ -86,6 +85,16 @@
         @pl.when(jnp.logical_not(diagonal))
         def _():
             pl.semaphore_signal(bar, inc=1, device_id=partner_z(d), device_id_type=MESH)
+
+    lax.fori_loop(1, 16, greet, 0)
+    pl.semaphore_signal(bar, inc=1, device_id=sibling, device_id_type=MESH)
+
+    @pl.when(jnp.logical_not(diagonal))
+    def _():
+        pl.semaphore_signal(bar, inc=1, device_id=partner, device_id_type=MESH)
+
+    for load in small:
+        load.wait()
 
     latent = comp_ref[:LAT, :].astype(jnp.float32).T
     normed = latent * lax.rsqrt(jnp.mean(latent * latent, axis=-1, keepdims=True) + 1e-06) * gain_ref[...]
@@ -462,9 +471,12 @@
     return pl.pallas_call(
         kernel,
         out_shape=jax.ShapeDtypeStruct((COLS, ROWS), bf16),
-        in_specs=[any_space, vmem, any_space, any_space, vmem, vmem],
+        in_specs=[any_space] * 6,
         out_specs=vmem,
         scratch_shapes=[
+            pltpu.VMEM((LAT + ROPE, ROWS), bf16),
+            pltpu.VMEM((1, ROWS), jnp.int32),
+            pltpu.VMEM((1, LAT), f32),
             pltpu.VMEM((NZ * 2 * ROWS, WIDE), bf16),
             pltpu.VMEM((HEADS_DEV, ROWS, 256), bf16),
             pltpu.VMEM((ROWS, HEADS_DEV * QK), bf16),
@@ -486,7 +498,7 @@
             dma((2, NZ)), dma((2, NZ)),
             dma, dma,
             dma, dma,
-            dma((3,)),
+            dma((6,)),
             dma((2, CHUNKS, 4)), dma((2, CHUNKS, 4)),
             dma((CHUNKS,)), dma((CHUNKS,)),
             dma((NZ, 3)), dma((NZ, 3)),

time: 77.2 us -> 76.4 us (0.990)
  Pallas kernels: 75.5 us -> 74.7 us
    pallas_call x1, Pallas kernels: 75.5 us -> 74.7 us  [per_device(): pl.pallas_call(kernel, out_shape=jax.ShapeDtypeStruct((COLS, ROWS), bf16)...]
where the time goes in v4:
time: 76.4 us; the launch traced here: 76.2 us
  Pallas kernels  74.7 us (98%)
  local copies, waits for them, and re-layouts  1.55 us (2%)
    pallas_call x1, Pallas kernels, per_device(): pl.pallas_call(kernel, out_shape=jax.ShapeDtypeStruct((COLS, ROWS), bf16)...  74.7 us
    unnamed x1, local copies, waits for them, and re-layouts  1.55 us

profile of v4, /device:TPU:6, one launch (start us, length us, event | category | flops | bytes accessed | tf_op | source)
XLA Modules:
  0.0 76.2 jit_solution(10351466311688205344)
XLA Ops:
  0.0 74.7 %prefill.1 = bf16[448,128]{1,0:T(8,128)(2,1)} custom-call(bf16[128,1536]{1,0:T(8,128)(2,1)} %q_hbm.1, bf16[576,128]{1,0:T(8,128)(2,1)} %bitcast.7, bf16[512,2048]{1,0:T(8,128)(2,1)} %kv_hbm.1, bf16[448,1024]{1,0:T(8,128)(2,1)} %bitcast.5, s32[1,128]{1,0:T(1,128)} %bitcast.9, f32[1,512]{1,0:T(1,128)} %bitcast.8), custom_call_target="tpu_custom_call" | custom-call | tf_op jit(solution)/shard_map/prefill/pallas_call | solution.py:471
  74.7 1.6 %copy.8 = bf16[128,448]{0,1:T(8,128)(2,1)} copy(bf16[128,448]{0,1:T(8,128)(2,1)} %bitcast.6) | data formatting | bytes 229376

commit v5 on v4

--- a/solution.py
+++ b/solution.py
@@ -291,8 +291,9 @@
         def _():
             full[p, own, :] = att[p]
 
-        @pl.when(jnp.logical_not(diagonal))
-        def _():
+    @pl.when(jnp.logical_not(diagonal))
+    def _():
+        for p in range(CHUNKS):
             swap(p).start()
 
     @pl.when(diagonal)
@@ -304,13 +305,8 @@
         w_swap.wait_recv()
 
     w_share.start()
-    pass_on(0, 1)
-    pass_on(1, 1)
-
-    @pl.when(jnp.logical_not(diagonal))
-    def _():
-        for p in range(CHUNKS):
-            swap(p).wait_recv()
+    for p in range(CHUNKS):
+        pass_on(p, 1)
 
     u = jnp.where(b == 0, y, x)
     v = jnp.where(b == 0, x, y)
@@ -383,9 +379,14 @@
     def project_round(s):
         lax.fori_loop(2 * s - 1, 2 * s + 1, project, 0)
 
-    for p in (2, 3):
-        pass_on(p, 1)
+    pass_on(0, 2)
     w_share.wait_recv()
+
+    @pl.when(jnp.logical_not(diagonal))
+    def _():
+        for p in range(CHUNKS):
+            swap(p).wait_recv()
+
     project(0, 0)
 
     for n in range(NZ):
@@ -404,7 +405,6 @@
         for p in range(CHUNKS):
             swap(p).wait_send()
 
-    pass_on(0, 2)
     pass_on(1, 2)
     project_round(1)
     pass_on(2, 2)
@@ -413,15 +413,15 @@
     pass_on(1, 3)
     project_round(2)
     pass_on(2, 3)
+    lax.fori_loop(0, 3, sum_first, 0)
     pass_on(3, 3)
-    lax.fori_loop(0, 3, sum_first, 0)
+    project_round(3)
     pass_on(0, 4)
     pass_on(2, 4)
-    project_round(3)
+    lax.fori_loop(3, 5, sum_first, 0)
+    lax.fori_loop(0, 3, sum_second, 0)
     pass_on(1, 4)
     pass_on(3, 4)
-    lax.fori_loop(3, 5, sum_first, 0)
-    lax.fori_loop(0, 3, sum_second, 0)
     project(7, 0)
     w_share.wait_send()
     for p in range(CHUNKS):

time: 76.4 us -> 75.7 us (level)
  no operation moved by 1% of the time
where the time goes in v5:
time: 75.7 us; the launch traced here: 75.5 us
  Pallas kernels  74 us (98%)
  local copies, waits for them, and re-layouts  1.55 us (2%)
    pallas_call x1, Pallas kernels, per_device(): pl.pallas_call(kernel, out_shape=jax.ShapeDtypeStruct((COLS, ROWS), bf16)...  74 us
    unnamed x1, local copies, waits for them, and re-layouts  1.55 us

profile of v5, /device:TPU:6, one launch (start us, length us, event | category | flops | bytes accessed | tf_op | source)
XLA Modules:
  0.0 75.5 jit_solution(1268515245236849936)
XLA Ops:
  0.0 74.0 %prefill.1 = bf16[448,128]{1,0:T(8,128)(2,1)} custom-call(bf16[128,1536]{1,0:T(8,128)(2,1)} %q_hbm.1, bf16[576,128]{1,0:T(8,128)(2,1)} %bitcast.7, bf16[512,2048]{1,0:T(8,128)(2,1)} %kv_hbm.1, bf16[448,1024]{1,0:T(8,128)(2,1)} %bitcast.5, s32[1,128]{1,0:T(1,128)} %bitcast.9, f32[1,512]{1,0:T(1,128)} %bitcast.8), custom_call_target="tpu_custom_call" | custom-call | tf_op jit(solution)/shard_map/prefill/pallas_call | solution.py:471
  74.0 1.6 %copy.8 = bf16[128,448]{0,1:T(8,128)(2,1)} copy(bf16[128,448]{0,1:T(8,128)(2,1)} %bitcast.6) | data formatting | bytes 229376

commit v6 on v5

--- a/solution.py
+++ b/solution.py
@@ -455,7 +455,7 @@
         def _():
             remote(sum2.at[0], result.at[pl.ds(n * 16, 16)], last_send.at[0], last_recv.at[n], sibling).wait_recv()
 
-    out_ref[...] = result[...].astype(jnp.float32).T.astype(jnp.bfloat16)
+    out_ref[...] = result[...]
 
     for n in range(NZ):
         @pl.when(jnp.logical_not(stays(n)))
@@ -470,7 +470,7 @@
     vmem = pl.BlockSpec(memory_space=pltpu.VMEM)
     return pl.pallas_call(
         kernel,
-        out_shape=jax.ShapeDtypeStruct((COLS, ROWS), bf16),
+        out_shape=jax.ShapeDtypeStruct((ROWS, COLS), bf16),
         in_specs=[any_space] * 6,
         out_specs=vmem,
         scratch_shapes=[
@@ -509,7 +509,7 @@
             collective_id=0, has_side_effects=True, vmem_limit_bytes=56 * 1024 * 1024
         ),
         name="prefill",
-    )(queries, compressed.T, kv_up, w_out.T, positions.reshape(1, ROWS), latent_gain.reshape(1, LAT)).T
+    )(queries, compressed.T, kv_up, w_out.T, positions.reshape(1, ROWS), latent_gain.reshape(1, LAT))
 
 
 def solution(mesh):

time: 75.7 us -> 75.7 us (level)
    pallas_call x0 -> x1, local copies, waits for them, and re-layouts: none -> 1.67 us  [per_device(): pl.pallas_call(kernel, out_shape=jax.ShapeDtypeStruct((ROWS, COLS), bf16)...]
    unnamed x1 -> x0, local copies, waits for them, and re-layouts: 1.55 us -> none
where the time goes in v6:
time: 75.7 us; the launch traced here: 75.6 us
  Pallas kernels  73.9 us (98%)
  local copies, waits for them, and re-layouts  1.67 us (2%)
    pallas_call x1, Pallas kernels, per_device(): pl.pallas_call(kernel, out_shape=jax.ShapeDtypeStruct((ROWS, COLS), bf16)...  73.9 us
    pallas_call x1, local copies, waits for them, and re-layouts, per_device(): pl.pallas_call(kernel, out_shape=jax.ShapeDtypeStruct((ROWS, COLS), bf16)...  1.67 us

profile of v6, /device:TPU:6, one launch (start us, length us, event | category | flops | bytes accessed | tf_op | source)
XLA Modules:
  0.0 75.6 jit_solution(17114060662647010654)
XLA Ops:
  0.0 73.9 %prefill.1 = bf16[128,448]{1,0:T(8,128)(2,1)} custom-call(bf16[128,1536]{1,0:T(8,128)(2,1)} %q_hbm.1, bf16[576,128]{1,0:T(8,128)(2,1)} %bitcast.5, bf16[512,2048]{1,0:T(8,128)(2,1)} %kv_hbm.1, bf16[448,1024]{1,0:T(8,128)(2,1)} %bitcast.4, s32[1,128]{1,0:T(1,128)} %bitcast.7, f32[1,512]{1,0:T(1,128)} %bitcast.6), custom_call_target="tpu_custom_call" | custom-call | tf_op jit(solution)/shard_map/prefill/pallas_call | solution.py:471
  73.9 1.7 %copy.7 = bf16[128,448]{0,1:T(8,128)(2,1)} copy(bf16[128,448]{1,0:T(8,128)(2,1)} %prefill.1) | data formatting | bytes 229376 | tf_op jit(solution)/shard_map/prefill/pallas_call | solution.py:471
